TPU v7x, 128 devices: a whole 4x4x4 slice. The times are simulated.
128 devices in a mesh: grp: 8 (over x, core), tp: 16 (over z, y).
Axes of the slice: x: 4, y: 4, z: 4, core: 2. Of those that a mesh axis runs over, the one named last changes fastest.
Arguments:
- activations: bfloat16 [4096, 8192], P('grp', 'tp'), may hold values from -6 to 6
- output_gradient: bfloat16 [4096, 8192], P('grp', 'tp'), may hold values from -6 to 6
- frozen_weight: bfloat16 [8192, 8192], P(None, 'tp'), may hold values from -0.0625 to 0.0625
- adapter_down_factors: bfloat16 [128, 32, 8192], P('grp', None, 'tp'), may hold values from -6 to 6
- adapter_up_factors: bfloat16 [128, 32, 8192], P('grp', None, 'tp'), may hold values from -6 to 6
- first_moment_down: float32 [128, 32, 8192], P('grp', None, 'tp'), may hold values from -6 to 6
- second_moment_down: float32 [128, 32, 8192], P('grp', None, 'tp'), may hold values from 0.5 to 2
- first_moment_up: float32 [128, 32, 8192], P('grp', None, 'tp'), may hold values from -6 to 6
- second_moment_up: float32 [128, 32, 8192], P('grp', None, 'tp'), may hold values from 0.5 to 2
- sample_row_prompt: int32 [8, 512], P('grp'), may hold values from 0 to 15, never falling along the last dimension, each value on 1 to 128 neighbouring positions
- majority_vote_reward: int32 [8, 512], P('grp'), may hold values 0 or 1
- prompt_adapter_slot: int32 [128], replicated, may hold values from 0 to 127, as said below
Outputs:
- layer_out: bfloat16 [4096, 8192], P('grp', 'tp')
- input_grad: bfloat16 [4096, 8192], P('grp', 'tp')
- updated_down_factors: bfloat16 [128, 32, 8192], P('grp', None, 'tp')
- updated_up_factors: bfloat16 [128, 32, 8192], P('grp', None, 'tp')
- updated_first_down: float32 [128, 32, 8192], P('grp', None, 'tp')
- updated_second_down: float32 [128, 32, 8192], P('grp', None, 'tp')
- updated_first_up: float32 [128, 32, 8192], P('grp', None, 'tp')
- updated_second_up: float32 [128, 32, 8192], P('grp', None, 'tp')
Inputs may be any that keep to these rules, and one draw needn't show every extreme that they name: `prompt_adapter_slot`: A permutation. Slots g * 16 to (g + 1) * 16 - 1 lie in group g's shard, and each group's shard holds the slots of exactly 2 prompts of every group.
All inputs are finite; a program needn't handle non-finite values. No bound on the sum of `majority_vote_reward` on one device may be relied on, other than what follows from the above.
Results may differ from a plain program's by a relative error of at most 0.0056.
Values may be sent and summed in bfloat16 or wider, within the bound.
No kernel may reach another device: no remote copies, remote signals or barrier semaphores. Data moves between devices by JAX's collectives and lax.ppermute only.
A program may use at most 192 MiB of HBM per device.

v0:
```python
import jax
import jax.numpy as jnp
from jax import lax
from jax.sharding import PartitionSpec as P

beta_first = 0.9
beta_second = 0.999
step_rate = 0.2
adam_eps = 1e-08
adapter_scale = 2.0


def moment_step_update(param, moment, second, grad):
    moment_new = beta_first * moment + (1.0 - beta_first) * grad
    second_new = beta_second * second + (1.0 - beta_second) * grad * grad
    param_new = param.astype(jnp.float32) - step_rate * moment_new / (
        jnp.sqrt(second_new) + adam_eps
    )
    return (param_new.astype(jnp.bfloat16), moment_new, second_new)


def local(
    activations,
    output_gradient,
    frozen_weight,
    adapter_down_factors,
    adapter_up_factors,
    first_moment_down,
    second_moment_down,
    first_moment_up,
    second_moment_up,
    sample_row_prompt,
    majority_vote_reward,
    prompt_adapter_slot,
):
    width = frozen_weight.shape[0]
    local_width = frozen_weight.shape[1]
    row_count = activations.shape[0]
    adapter_slot_count = adapter_down_factors.shape[0]
    adapter_rank_size = adapter_down_factors.shape[1]
    prompt_count = prompt_adapter_slot.shape[0]
    member = lax.axis_index("grp")
    scale_down = width ** (-0.5)
    scaled_up_factors = adapter_scale / adapter_rank_size**0.5
    contract_cols = (((1,), (1,)), ((), ()))
    contract_rows = (((0,), (0,)), ((), ()))
    labels = sample_row_prompt[0]
    onehot = (labels[:, None] == jnp.arange(adapter_slot_count, dtype=jnp.int32)[None, :]).astype(
        jnp.float32
    )
    reward = majority_vote_reward[0].astype(jnp.float32)
    counts = jnp.sum(onehot, axis=0)
    mean_reward = jnp.sum(onehot * reward[:, None], axis=0) / counts
    advantage = reward - jnp.sum(onehot * mean_reward[None, :], axis=1)
    weighted = (advantage[:, None] * output_gradient.astype(jnp.float32)).astype(jnp.bfloat16)
    my_slots = lax.dynamic_slice_in_dim(
        prompt_adapter_slot, member * adapter_slot_count, adapter_slot_count
    )
    every_down, every_up = (
        lax.all_gather(adapter_down_factors, "grp", axis=0, tiled=True),
        lax.all_gather(adapter_up_factors, "grp", axis=0, tiled=True),
    )
    down_local = jnp.take(every_down, my_slots, axis=0)
    up_local = jnp.take(every_up, my_slots, axis=0)
    flattened_down = down_local.reshape(adapter_slot_count * adapter_rank_size, local_width)
    flattened_up = up_local.reshape(adapter_slot_count * adapter_rank_size, local_width)
    low_all = lax.dot_general(
        activations, flattened_down, contract_cols, preferred_element_type=jnp.float32
    )
    low_part = jnp.sum(
        low_all.reshape(row_count, adapter_slot_count, adapter_rank_size) * onehot[:, :, None],
        axis=1,
    )
    back_all = lax.dot_general(
        weighted, flattened_up, contract_cols, preferred_element_type=jnp.float32
    )
    back_part = jnp.sum(
        back_all.reshape(row_count, adapter_slot_count, adapter_rank_size) * onehot[:, :, None],
        axis=1,
    )
    low_sum, back_sum = lax.psum((low_part, back_part), "tp")
    base_out = jnp.dot(
        lax.all_gather(activations, "tp", axis=1, tiled=True),
        frozen_weight,
        preferred_element_type=jnp.float32,
    )
    low = (scale_down * low_sum).astype(jnp.bfloat16)
    back_low = (scaled_up_factors * back_sum).astype(jnp.bfloat16)
    onehot_half = onehot.astype(jnp.bfloat16)
    low_wide = (onehot_half[:, :, None] * low[:, None, :]).reshape(
        row_count, adapter_slot_count * adapter_rank_size
    )
    back_wide = (onehot_half[:, :, None] * back_low[:, None, :]).reshape(
        row_count, adapter_slot_count * adapter_rank_size
    )
    layer_out = (
        base_out
        + scaled_up_factors * jnp.dot(low_wide, flattened_up, preferred_element_type=jnp.float32)
    ).astype(jnp.bfloat16)
    full_back = lax.dot_general(
        weighted, frozen_weight, contract_cols, preferred_element_type=jnp.float32
    )
    input_sum = lax.psum_scatter(full_back, "tp", scatter_dimension=1, tiled=True)
    input_grad = (
        input_sum
        + scale_down * jnp.dot(back_wide, flattened_down, preferred_element_type=jnp.float32)
    ).astype(jnp.bfloat16)
    grad_down = scale_down * lax.dot_general(
        back_wide, activations, contract_rows, preferred_element_type=jnp.float32
    )
    grad_up = scaled_up_factors * lax.dot_general(
        low_wide, weighted, contract_rows, preferred_element_type=jnp.float32
    )
    grad_down = grad_down.astype(jnp.bfloat16).reshape(
        adapter_slot_count, adapter_rank_size, local_width
    )
    grad_up = grad_up.astype(jnp.bfloat16).reshape(
        adapter_slot_count, adapter_rank_size, local_width
    )
    holder_down = (
        jnp.zeros((prompt_count, adapter_rank_size, local_width), jnp.bfloat16)
        .at[my_slots]
        .set(grad_down)
    )
    holder_up = (
        jnp.zeros((prompt_count, adapter_rank_size, local_width), jnp.bfloat16)
        .at[my_slots]
        .set(grad_up)
    )
    down_factor_slot, up_factor_slot = (
        lax.psum_scatter(holder_down, "grp", scatter_dimension=0, tiled=True).astype(jnp.float32),
        lax.psum_scatter(holder_up, "grp", scatter_dimension=0, tiled=True).astype(jnp.float32),
    )
    updated_down_factors, updated_first_down, updated_second_down = moment_step_update(
        adapter_down_factors, first_moment_down, second_moment_down, down_factor_slot
    )
    updated_up_factors, updated_first_up, updated_second_up = moment_step_update(
        adapter_up_factors, first_moment_up, second_moment_up, up_factor_slot
    )
    return (
        layer_out,
        input_grad,
        updated_down_factors,
        updated_up_factors,
        updated_first_down,
        updated_second_down,
        updated_first_up,
        updated_second_up,
    )


def solution(mesh):
    in_specs = (
        P("grp", "tp"),
        P("grp", "tp"),
        P(None, "tp"),
        P("grp", None, "tp"),
        P("grp", None, "tp"),
        P("grp", None, "tp"),
        P("grp", None, "tp"),
        P("grp", None, "tp"),
        P("grp", None, "tp"),
        P("grp", None),
        P("grp", None),
        P(),
    )
    out_specs = (
        P("grp", "tp"),
        P("grp", "tp"),
        P("grp", None, "tp"),
        P("grp", None, "tp"),
        P("grp", None, "tp"),
        P("grp", None, "tp"),
        P("grp", None, "tp"),
        P("grp", None, "tp"),
    )
    return jax.shard_map(local, mesh=mesh, in_specs=in_specs, out_specs=out_specs, check_vma=False)
```

profile of v0, /device:TPU:1, one launch (start us, length us, event | category | flops | bytes accessed | tf_op | source)
XLA Modules:
  0.0 447.7 jit_solution(7492767387817051464)
XLA Ops:
  7.2 0.7 all-gather.6.cloned.1.call-update
  8.0 0.7 all-gather.8.cloned.1.call-update
  8.7 0.7 convert_element_type.76
  9.4 0.8 fusion.14
  10.2 0.8 select_reduce_fusion
  11.0 0.7 compare_and_fusion
  11.7 0.7 fusion.15
  12.4 33.0 %all-gather.6.cloned.1.call-done = bf16[128,32,512]{2,1,0:T(8,128)(2,1)} async-done(((bf16[16,32,512]{2,1,0:T(8,128)(2,1)}), bf16[128,32,512]{2,1,0:T(8,128)(2,1)}) %all-gather.6.cloned.1.call-update) | async-done | bytes 4194320 | tf_op jit(solution)/shard_map/all_gather | solution.py:60
  45.5 2.8 gather_fusion
  48.4 1.5 fusion.23
  49.9 0.8 multiply_reduce_fusion
  50.6 28.6 %all-gather.8.cloned.1.call-done = bf16[128,32,512]{2,1,0:T(8,128)(2,1)} async-done(((bf16[16,32,512]{2,1,0:T(8,128)(2,1)}), bf16[128,32,512]{2,1,0:T(8,128)(2,1)}) %all-gather.8.cloned.1.call-update) | async-done | bytes 4194320 | tf_op jit(solution)/shard_map/all_gather | solution.py:61
  79.3 2.8 gather_fusion.1
  82.0 2.3 fusion.7
  85.0 80.4 %all-reduce.3.cloned.1.call-done = (f32[512,32]{0,1:T(8,128)}, f32[512,32]{0,1:T(8,128)}) async-done(((f32[512,32]{0,1:T(8,128)}, f32[512,32]{0,1:T(8,128)}), (f32[512,32]{0,1:T(8,128)}, f32[512,32]{0,1:T(8,128)})) %all-reduce.3.cloned.1.call-update) | async-done | bytes 131088 | tf_op jit(solution)/shard_map/psum | solution.py:81
  165.4 0.8 multiply_convert_fusion.2
  166.2 0.8 multiply_convert_fusion.1
  167.6 2.5 broadcast.85.clone
  170.1 2.6 scatter_fusion
  172.7 0.5 fusion.5
  173.2 2.5 broadcast.85.clone.1
  175.7 2.6 scatter_fusion.1
  178.4 11.8 %fusion.18 = f32[512,8192]{1,0:T(8,128)} fusion(bf16[8192,512]{1,0:T(8,128)(2,1)} %param.16, bf16[512,512]{1,0:T(8,128)(2,1)S(1)} %copy-done.4, f32[512]{0:T(512)S(1)} %sub.13), kind=kOutput, calls=%fused_computation.48 | convolution fusion | flops 4295753728 | bytes 25692160 | tf_op jit(solution)/shard_map/dot_general | solution.py:100
  190.2 1.5 fusion.1
  191.7 54.1 %all-gather.4.cloned.1.call-done = bf16[512,8192]{1,0:T(8,128)(2,1)} async-done(((bf16[512,512]{1,0:T(8,128)(2,1)}), bf16[512,8192]{1,0:T(8,128)(2,1)}) %all-gather.4.cloned.1.call-update) | async-done | bytes 8388624 | tf_op jit(solution)/shard_map/all_gather | solution.py:83
  245.8 11.3 %fusion.6 = bf16[512,512]{1,0:T(8,128)(2,1)} fusion(f32[512,512]{1,0:T(8,128)} %fusion.1, bf16[512,8192]{1,0:T(8,128)(2,1)} %all-gather.4.cloned.1.call-done, bf16[8192,512]{1,0:T(8,128)(2,1)} %param.16), kind=kOutput, calls=%fused_computation.20 | convolution fusion | flops 4295491584 | bytes 18350080 | tf_op jit(solution)/shard_map/dot_general | solution.py:82
  257.1 26.1 %reduce-scatter.6.cloned.1.call-done = bf16[16,32,512]{2,1,0:T(8,128)(2,1)} async-done(((bf16[128,32,512]{2,1,0:T(8,128)(2,1)}), bf16[16,32,512]{2,1,0:T(8,128)(2,1)}) %reduce-scatter.6.cloned.1.call-update) | async-done | bytes 524304 | tf_op jit(solution)/shard_map/reduce_scatter | solution.py:131
  283.2 3.3 subtract_convert_fusion.1
  286.5 35.9 %reduce-scatter.8.cloned.1.call-done = bf16[16,32,512]{2,1,0:T(8,128)(2,1)} async-done(((bf16[128,32,512]{2,1,0:T(8,128)(2,1)}), bf16[16,32,512]{2,1,0:T(8,128)(2,1)}) %reduce-scatter.8.cloned.1.call-update) | async-done | bytes 524304 | tf_op jit(solution)/shard_map/reduce_scatter | solution.py:132
  322.4 3.6 subtract_convert_fusion
  326.1 112.3 %reduce-scatter.4.cloned.1.call-done = f32[512,512]{1,0:T(8,128)} async-done(((f32[512,8192]{1,0:T(8,128)}), f32[512,512]{1,0:T(8,128)}) %reduce-scatter.4.cloned.1.call-update) | async-done | bytes 1048592 | tf_op jit(solution)/shard_map/reduce_scatter | solution.py:103
  438.3 2.5 fusion.3
  (28 shorter events, 1.5 us)
Async XLA Ops:
  7.2 160.0 %copy-start = (bf16[512,512]{1,0:T(8,128)(2,1)S(1)}, bf16[512,512]{1,0:T(8,128)(2,1)}, u32[]{:S(2)}) copy-start(bf16[512,512]{1,0:T(8,128)(2,1)} %param.14) | copy-start | bytes 1572868
  7.2 38.3 %all-gather.6.cloned.1.call-start = ((), (), s32[]{:S(2)}) async-start(), calls=%async_computation.4 | async-start | bytes 4718592 | tf_op jit(solution)/shard_map/all_gather | solution.py:60
  7.9 71.3 %all-gather.8.cloned.1.call-start = ((), (), s32[]{:S(2)}) async-start(), calls=%async_computation.5 | async-start | bytes 4718592 | tf_op jit(solution)/shard_map/all_gather | solution.py:61
  8.7 156.7 %all-reduce.3.cloned.1.call-start = ((), (), s32[]{:S(2)}) async-start(), calls=%async_computation.9 | async-start | bytes 262144 | tf_op jit(solution)/shard_map/psum | solution.py:81
  82.0 90.7 %copy-start.4 = (bf16[512,512]{1,0:T(8,128)(2,1)S(1)}, bf16[512,512]{1,0:T(8,128)(2,1)}, u32[]{:S(2)}) copy-start(bf16[512,512]{1,0:T(8,128)(2,1)} %param.15) | copy-start | bytes 1572868
  84.4 161.4 %all-gather.4.cloned.1.call-start = ((), (), s32[]{:S(2)}) async-start(), calls=%async_computation.3 | async-start | bytes 8912896 | tf_op jit(solution)/shard_map/all_gather | solution.py:83
  85.0 198.2 %reduce-scatter.6.cloned.1.call-start = ((), (), s32[]{:S(2)}) async-start(), calls=%async_computation.7 | async-start | bytes 4718592 | tf_op jit(solution)/shard_map/reduce_scatter | solution.py:131
  172.6 149.8 %reduce-scatter.8.cloned.1.call-start = ((), (), s32[]{:S(2)}) async-start(), calls=%async_computation.8 | async-start | bytes 4718592 | tf_op jit(solution)/shard_map/reduce_scatter | solution.py:132
  178.3 260.0 %reduce-scatter.4.cloned.1.call-start = ((), (), s32[]{:S(2)}) async-start(), calls=%async_computation.6 | async-start | bytes 17825792 | tf_op jit(solution)/shard_map/reduce_scatter | solution.py:103
  191.7 91.5 %copy-start.1 = (bf16[16,32,512]{2,1,0:T(8,128)(2,1)S(1)}, bf16[16,32,512]{2,1,0:T(8,128)(2,1)}, u32[]{:S(2)}) copy-start(bf16[16,32,512]{2,1,0:T(8,128)(2,1)} %param.17) | copy-start | bytes 1572868
  191.7 91.5 %copy-start.3 = (f32[16,32,512]{2,1,0:T(8,128)S(1)}, f32[16,32,512]{2,1,0:T(8,128)}, u32[]{:S(2)}) copy-start(f32[16,32,512]{2,1,0:T(8,128)} %param.19) | copy-start | bytes 3145732
  191.7 130.8 %copy-start.2 = (bf16[16,32,512]{2,1,0:T(8,128)(2,1)S(1)}, bf16[16,32,512]{2,1,0:T(8,128)(2,1)}, u32[]{:S(2)}) copy-start(bf16[16,32,512]{2,1,0:T(8,128)(2,1)} %param.18) | copy-start | bytes 1572868
Sparse Core Ops, SparseCore 0:
  9.7 35.6 all-gather.5
  47.2 32.0 all-gather.7
  84.5 80.8 all-reduce.2
  167.5 78.2 all-gather.3
  248.2 34.9 reduce-scatter.5
  285.6 36.8 reduce-scatter.7
  326.2 112.0 reduce-scatter.3
where the time goes:
time: 448 us
  waiting for transfers between devices  372 us (83%)
  matrix products  31.8 us (7%)
  local copies, waits for them, and re-layouts  15.6 us (3%)
  between operations  14.2 us (3%)
  other arithmetic  13.3 us (3%)
    reduce_scatter x1, waiting for transfers between devices, local(): lax.psum_scatter(full_back, 'tp', scatter_dimension=1, tiled=True)  112 us
    psum x1, waiting for transfers between devices, local(): low_sum, back_sum = lax.psum((low_part, back_part), 'tp')  80.4 us
    all_gather x1, waiting for transfers between devices, local(): lax.all_gather(activations, 'tp', axis=1, tiled=True)  54.1 us
    reduce_scatter x1, waiting for transfers between devices, local(): lax.psum_scatter(holder_up, 'grp', scatter_dimension=0, tiled=True)  35.9 us
    all_gather x1, waiting for transfers between devices, local(): lax.all_gather(adapter_down_factors, 'grp', axis=0, tiled=True)  33 us
    all_gather x1, waiting for transfers between devices, local(): lax.all_gather(adapter_up_factors, 'grp', axis=0, tiled=True)  28.6 us
    reduce_scatter x1, waiting for transfers between devices, local(): lax.psum_scatter(holder_down, 'grp', scatter_dimension=0, tiled=True)  26.1 us
    dot_general x1, matrix products, local(): lax.dot_general(weighted, frozen_weight, contract_cols, preferred_element...  11.8 us
  transfers between devices with their start and end apart: 7, of which 7 were waited for; matrix products, arithmetic and copies ran while one was open for 12% of the time, Pallas kernels for 0%

commit v1 on v0

--- a/solution.py
+++ b/solution.py
@@ -8,6 +8,13 @@
 step_rate = 0.2
 adam_eps = 1e-08
 adapter_scale = 2.0
+
+
+def form_arrays_up(chunk, axis_key):
+    finding = jax.lax.psum(1, axis_name=axis_key)
+    raw_out = jnp.stack(finding * [chunk], 0)
+    local_part = jax.lax.all_to_all(raw_out, axis_name=axis_key, split_axis=0, concat_axis=0)
+    return jnp.concatenate(local_part, 1)
 
 
 def moment_step_update(param, moment, second, grad):
@@ -80,9 +87,7 @@
     )
     low_sum, back_sum = lax.psum((low_part, back_part), "tp")
     base_out = jnp.dot(
-        lax.all_gather(activations, "tp", axis=1, tiled=True),
-        frozen_weight,
-        preferred_element_type=jnp.float32,
+        form_arrays_up(activations, "tp"), frozen_weight, preferred_element_type=jnp.float32
     )
     low = (scale_down * low_sum).astype(jnp.bfloat16)
     back_low = (scaled_up_factors * back_sum).astype(jnp.bfloat16)

time: 448 us -> 426 us (0.951)
  waiting for transfers between devices: 372 us -> 341 us
  starting transfers between devices: 0.28 us -> 5.17 us
    all_to_all x0 -> x1, waiting for transfers between devices: none -> 131 us  [form_arrays_up(): jax.lax.all_to_all(raw_out, axis_name=axis_key, split_axis=0, concat_axis=0)]
    all_gather x1 -> x0, waiting for transfers between devices: 54.1 us -> none  [local(): lax.all_gather(activations, 'tp', axis=1, tiled=True)]
    reduce_scatter x1, waiting for transfers between devices: 112 us -> 66 us  [local(): lax.psum_scatter(full_back, 'tp', scatter_dimension=1, tiled=True)]
    reduce_scatter x1, waiting for transfers between devices: 35.9 us -> 0.01 us  [local(): lax.psum_scatter(holder_up, 'grp', scatter_dimension=0, tiled=True)]
    reduce_scatter x1, waiting for transfers between devices: 26.1 us -> 0.01 us  [local(): lax.psum_scatter(holder_down, 'grp', scatter_dimension=0, tiled=True)]
    all_to_all x0 -> x1, starting transfers between devices: none -> 4.94 us  [form_arrays_up(): jax.lax.all_to_all(raw_out, axis_name=axis_key, split_axis=0, concat_axis=0)]
    another operation x2 -> x3, local copies, waits for them, and re-layouts: 4.94 us -> 9.07 us
  transfers between devices with their start and end apart: 7 -> 7, of which waited for: 7 -> 5; matrix products, arithmetic and copies ran while one was open for 12% -> 12% of each run, Pallas kernels for 0% -> 0%
where the time goes in v1:
time: 426 us
  waiting for transfers between devices  341 us (80%)
  matrix products  32.2 us (8%)
  local copies, waits for them, and re-layouts  20 us (5%)
  between operations  14.2 us (3%)
  other arithmetic  13.4 us (3%)
  starting transfers between devices  5.17 us (1%)
    all_to_all x1, waiting for transfers between devices, form_arrays_up(): jax.lax.all_to_all(raw_out, axis_name=axis_key, split_axis=0, concat_axis=0)  131 us
    psum x1, waiting for transfers between devices, local(): low_sum, back_sum = lax.psum((low_part, back_part), 'tp')  80.9 us
    reduce_scatter x1, waiting for transfers between devices, local(): lax.psum_scatter(full_back, 'tp', scatter_dimension=1, tiled=True)  66 us
    all_gather x1, waiting for transfers between devices, local(): lax.all_gather(adapter_down_factors, 'grp', axis=0, tiled=True)  33 us
    all_gather x1, waiting for transfers between devices, local(): lax.all_gather(adapter_up_factors, 'grp', axis=0, tiled=True)  28.6 us
    dot_general x1, matrix products, local(): lax.dot_general(weighted, frozen_weight, contract_cols, preferred_element...  11.8 us
    dot_general x1, matrix products, local(): jnp.dot(form_arrays_up(activations, 'tp'), frozen_weight, preferred_eleme...  11.7 us
  transfers between devices with their start and end apart: 7, of which 5 were waited for; matrix products, arithmetic and copies ran while one was open for 12% of the time, Pallas kernels for 0%

profile of v1, /device:TPU:1, one launch (start us, length us, event | category | flops | bytes accessed | tf_op | source)
XLA Modules:
  0.0 425.6 jit_solution(1518150475210743654)
XLA Ops:
  7.2 0.7 all-gather.3.cloned.1.call-update
  8.0 0.7 all-gather.5.cloned.1.call-update
  8.7 0.7 convert_element_type.76
  9.4 0.8 fusion.14
  10.2 0.8 select_reduce_fusion
  11.0 0.7 compare_and_fusion
  11.7 0.7 fusion.15
  12.4 33.0 %all-gather.3.cloned.1.call-done = bf16[128,32,512]{2,1,0:T(8,128)(2,1)} async-done(((bf16[16,32,512]{2,1,0:T(8,128)(2,1)}), bf16[128,32,512]{2,1,0:T(8,128)(2,1)}) %all-gather.3.cloned.1.call-update) | async-done | bytes 4194320 | tf_op jit(solution)/shard_map/all_gather | solution.py:67
  45.5 2.8 gather_fusion
  48.4 1.5 fusion.23
  49.9 0.8 multiply_reduce_fusion
  50.6 28.6 %all-gather.5.cloned.1.call-done = bf16[128,32,512]{2,1,0:T(8,128)(2,1)} async-done(((bf16[16,32,512]{2,1,0:T(8,128)(2,1)}), bf16[128,32,512]{2,1,0:T(8,128)(2,1)}) %all-gather.5.cloned.1.call-update) | async-done | bytes 4194320 | tf_op jit(solution)/shard_map/all_gather | solution.py:68
  79.3 2.8 gather_fusion.1
  82.0 2.2 fusion.7
  84.4 80.9 %all-reduce.3.cloned.1.call-done = (f32[512,32]{0,1:T(8,128)}, f32[512,32]{0,1:T(8,128)}) async-done(((f32[512,32]{0,1:T(8,128)}, f32[512,32]{0,1:T(8,128)}), (f32[512,32]{0,1:T(8,128)}, f32[512,32]{0,1:T(8,128)})) %all-reduce.3.cloned.1.call-update) | async-done | bytes 131088 | tf_op jit(solution)/shard_map/psum | solution.py:88
  165.3 0.8 multiply_convert_fusion.2
  166.1 0.8 multiply_convert_fusion.1
  167.5 2.6 broadcast.87.clone
  170.1 2.6 scatter_fusion
  172.8 0.5 fusion.6
  173.3 2.5 broadcast.87.clone.1
  175.8 2.6 scatter_fusion.1
  178.4 11.8 %fusion.18 = f32[512,8192]{1,0:T(8,128)} fusion(bf16[8192,512]{1,0:T(8,128)(2,1)} %param.16, bf16[512,512]{1,0:T(8,128)(2,1)S(1)} %copy-done.4, f32[512]{0:T(512)S(1)} %sub.13), kind=kOutput, calls=%fused_computation.48 | convolution fusion | flops 4295753728 | bytes 25692160 | tf_op jit(solution)/shard_map/dot_general | solution.py:105
  190.5 4.0 stack.2
  194.5 4.9 %all-to-all-start = ((bf16[16,512,512]{1,2,0:T(8,128)(2,1)}), bf16[16,512,512]{1,2,0:T(8,128)(2,1)}, u32[]{:S(2)}, u32[]{:S(2)}) async-start(bf16[16,512,512]{1,2,0:T(8,128)(2,1)} %stack.2), calls=%async_computation | async-start | bytes 16777216 | tf_op jit(solution)/shard_map/all_to_all | solution.py:16
  199.4 1.5 fusion.1
  200.9 130.5 %all-to-all-done = bf16[16,512,512]{1,2,0:T(8,128)(2,1)} async-done(((bf16[16,512,512]{1,2,0:T(8,128)(2,1)}), bf16[16,512,512]{1,2,0:T(8,128)(2,1)}, u32[]{:S(2)}, u32[]{:S(2)}) %all-to-all-start) | async-done | bytes 8388640 | tf_op jit(solution)/shard_map/all_to_all | solution.py:16
  331.4 11.7 %fusion.3 = bf16[512,512]{1,0:T(8,128)(2,1)} fusion(f32[512,512]{1,0:T(8,128)} %fusion.1, bf16[512,8192]{0,1:T(8,128)(2,1)} %bitcast.1, bf16[8192,512]{1,0:T(8,128)(2,1)} %param.16), kind=kOutput, calls=%fused_computation.17 | convolution fusion | flops 4295491584 | bytes 18350080 | tf_op jit(solution)/shard_map/dot_general | solution.py:89
  343.2 3.3 subtract_convert_fusion.1
  346.5 3.7 subtract_convert_fusion
  350.3 66.0 %reduce-scatter.4.cloned.1.call-done = f32[512,512]{1,0:T(8,128)} async-done(((f32[512,8192]{1,0:T(8,128)}), f32[512,512]{1,0:T(8,128)}) %reduce-scatter.4.cloned.1.call-update) | async-done | bytes 1048592 | tf_op jit(solution)/shard_map/reduce_scatter | solution.py:108
  416.3 2.5 fusion.4
  (29 shorter events, 1.2 us)
Async XLA Ops:
  7.2 159.9 %copy-start = (bf16[512,512]{1,0:T(8,128)(2,1)S(1)}, bf16[512,512]{1,0:T(8,128)(2,1)}, u32[]{:S(2)}) copy-start(bf16[512,512]{1,0:T(8,128)(2,1)} %param.14) | copy-start | bytes 1572868
  7.2 38.3 %all-gather.3.cloned.1.call-start = ((), (), s32[]{:S(2)}) async-start(), calls=%async_computation.4 | async-start | bytes 4718592 | tf_op jit(solution)/shard_map/all_gather | solution.py:67
  7.9 71.3 %all-gather.5.cloned.1.call-start = ((), (), s32[]{:S(2)}) async-start(), calls=%async_computation.5 | async-start | bytes 4718592 | tf_op jit(solution)/shard_map/all_gather | solution.py:68
  8.7 156.6 %all-reduce.3.cloned.1.call-start = ((), (), s32[]{:S(2)}) async-start(), calls=%async_computation.9 | async-start | bytes 262144 | tf_op jit(solution)/shard_map/psum | solution.py:88
  50.6 122.1 %copy-start.4 = (bf16[512,512]{1,0:T(8,128)(2,1)S(1)}, bf16[512,512]{1,0:T(8,128)(2,1)}, u32[]{:S(2)}) copy-start(bf16[512,512]{1,0:T(8,128)(2,1)} %param.15) | copy-start | bytes 1572868
  84.3 258.9 %reduce-scatter.6.cloned.1.call-start = ((), (), s32[]{:S(2)}) async-start(), calls=%async_computation.7 | async-start | bytes 4718592 | tf_op jit(solution)/shard_map/reduce_scatter | solution.py:136
  172.7 173.8 %reduce-scatter.8.cloned.1.call-start = ((), (), s32[]{:S(2)}) async-start(), calls=%async_computation.8 | async-start | bytes 4718592 | tf_op jit(solution)/shard_map/reduce_scatter | solution.py:137
  178.4 237.9 %reduce-scatter.4.cloned.1.call-start = ((), (), s32[]{:S(2)}) async-start(), calls=%async_computation.6 | async-start | bytes 17825792 | tf_op jit(solution)/shard_map/reduce_scatter | solution.py:108
  194.5 137.0 %all-to-all-start = ((bf16[16,512,512]{1,2,0:T(8,128)(2,1)}), bf16[16,512,512]{1,2,0:T(8,128)(2,1)}, u32[]{:S(2)}, u32[]{:S(2)}) async-start(bf16[16,512,512]{1,2,0:T(8,128)(2,1)} %stack.2), calls=%async_computation | async-start | bytes 16777216 | tf_op jit(solution)/shard_map/all_to_all | solution.py:16
  331.4 11.8 %copy-start.1 = (bf16[16,32,512]{2,1,0:T(8,128)(2,1)S(1)}, bf16[16,32,512]{2,1,0:T(8,128)(2,1)}, u32[]{:S(2)}) copy-start(bf16[16,32,512]{2,1,0:T(8,128)(2,1)} %param.17) | copy-start | bytes 1572868
  331.4 11.8 %copy-start.3 = (f32[16,32,512]{2,1,0:T(8,128)S(1)}, f32[16,32,512]{2,1,0:T(8,128)}, u32[]{:S(2)}) copy-start(f32[16,32,512]{2,1,0:T(8,128)} %param.19) | copy-start | bytes 3145732
  331.4 15.1 %copy-start.2 = (bf16[16,32,512]{2,1,0:T(8,128)(2,1)S(1)}, bf16[16,32,512]{2,1,0:T(8,128)(2,1)}, u32[]{:S(2)}) copy-start(bf16[16,32,512]{2,1,0:T(8,128)(2,1)} %param.18) | copy-start | bytes 1572868
Sparse Core Ops, SparseCore 0:
  9.7 35.6 all-gather.2
  47.2 32.0 all-gather.4
  84.4 80.8 all-reduce.2
  172.8 35.4 reduce-scatter.5
  210.7 37.7 reduce-scatter.7
  252.1 164.1 reduce-scatter.3
